TPU v7x, 32 devices: a whole 2x2x4 slice. The times are simulated.
32 devices in a mesh: seq: 8 (over y, x, core), chan: 4 (over z).
Axes of the slice: x: 2, y: 2, z: 4, core: 2. Of those that a mesh axis runs over, the one named last changes fastest.
Arguments:
- out_grad: bfloat16 [4096, 8192], P('seq', 'chan'), may hold values from -6 to 6
- out_weight: bfloat16 [1024, 8192], P(None, 'chan'), may hold values from -0.0625 to 0.0625
- conv_input: bfloat16 [1024, 4096], P('chan', 'seq'), may hold values from -6 to 6
- gate_values: bfloat16 [1024, 4096], P('chan', 'seq'), may hold values from -6 to 6
- conv_output: bfloat16 [1024, 4096], P('chan', 'seq'), may hold values from -6 to 6
- filters: bfloat16 [2, 1024, 512], P(None, 'chan'), may hold values from -0.29882812 to 0.29882812
- filter_reach: int32 [16], replicated, may hold values from 128 to 512, as said below
Outputs:
- grad_input: float32 [1024, 4096], P('chan', 'seq')
- grad_gate: float32 [1024, 4096], P('chan', 'seq')
- grad_weight: float32 [1024, 8192], P('seq', 'chan')
- grad_filters: float32 [2, 1024, 512], P(None, 'chan', 'seq')
Inputs may be any that keep to these rules, and one draw needn't show every extreme that they name: `filter_reach`: group g holds channels g * 64 to (g + 1) * 64 - 1. Every reach is a multiple of 128, and at least one group has reach 512.
All inputs are finite; a program needn't handle non-finite values.
Results may differ from a plain program's by a relative error of at most 0.014.
Values may be sent and summed in bfloat16 or wider, within the bound.
A program may use at most 128 MiB of HBM per device.

v0:
```python
import math

import jax
import jax.numpy as jnp
from jax import lax
from jax.experimental import pallas as pl
from jax.experimental.pallas import tpu as pltpu
from jax.sharding import PartitionSpec as P

GROUP = 64
LANES = 128
STEP = 8


def extended(block, sides, width):
    for axis, dim in sides:
        count = lax.axis_size(axis)
        forward = [(i, i + 1) for i in range(count - 1)]
        backward = [(target, source) for source, target in forward]
        low = lax.ppermute(
            lax.slice_in_dim(block, block.shape[dim] - width, None, axis=dim), axis, forward
        )
        high = lax.ppermute(lax.slice_in_dim(block, 0, width, axis=dim), axis, backward)
        block = jnp.concatenate([low, block, high], axis=dim)
    return block


def correlate_kernel(grad_ref, taps_ref, input_ref, out_ref, tiles_ref, lines_ref):
    channels = grad_ref.shape[0]
    span, tok_len = taps_ref.shape[1], input_ref.shape[1]
    out_blocks, tap_blocks = tok_len // LANES, span // LANES
    tile_count = tiles_ref.shape[1] // LANES
    row = lax.broadcasted_iota(jnp.int32, (LANES, LANES), 0)
    lane = lax.broadcasted_iota(jnp.int32, (LANES, LANES), 1)
    first = lane <= row
    rows = out_ref.shape[1]

    @pl.when(pl.program_id(0) == 0)
    def _():
        lines_ref[...] = jnp.zeros_like(lines_ref)

    for pair in range(channels // 2):
        for half in range(2):
            channel = 2 * pair + half

            def rolled(window):
                line = grad_ref[channel : channel + 1, window * LANES : (window + 1) * LANES]
                spread = jnp.broadcast_to(line, (LANES, LANES))
                return pltpu.roll(spread, 1, 1, stride=1, stride_axis=0)

            current = rolled(0)
            for tile in range(tile_count):
                following = rolled(tile + 1)
                tiles_ref[
                    pair % 2, tile * LANES : (tile + 1) * LANES, half * LANES : (half + 1) * LANES
                ] = jnp.where(first, current, following).astype(jnp.bfloat16)
                current = following
            top = half * rows
            for a in range(out_blocks):
                lines_ref[pair % 2, top + a : top + a + 1, a * LANES : a * LANES + span] = taps_ref[
                    channel : channel + 1, :
                ]
            top = top + out_blocks
            for b in range(tap_blocks):
                lines_ref[pair % 2, top + b : top + b + 1, b * LANES : b * LANES + tok_len] = (
                    input_ref[channel : channel + 1, :]
                )
        product = jnp.dot(
            lines_ref[pair % 2].astype(jnp.bfloat16),
            tiles_ref[pair % 2],
            preferred_element_type=jnp.float32,
        )
        out_ref[2 * pair] = product[:rows, :LANES]
        out_ref[2 * pair + 1] = product[rows:, LANES:]


def filter_terms(grad_ext, conv_input, kernel_taps):
    channels, tok_len = conv_input.shape
    span = kernel_taps.shape[1]
    out_blocks = tok_len // LANES
    tap_blocks = span // LANES
    tile_count = out_blocks + tap_blocks - 1
    depth = tile_count * LANES
    rows = -(-(out_blocks + tap_blocks) // 16) * 16

    def turned(array):
        return array.reshape(channels, -1, LANES)[:, :, ::-1].reshape(channels, -1).astype(jnp.float32)

    out = pl.pallas_call(
        correlate_kernel,
        grid=(channels // STEP,),
        out_shape=jax.ShapeDtypeStruct((channels, rows, LANES), jnp.float32),
        in_specs=[
            pl.BlockSpec((STEP, grad_ext.shape[1]), lambda i: (i, 0)),
            pl.BlockSpec((STEP, span), lambda i: (i, 0)),
            pl.BlockSpec((STEP, tok_len), lambda i: (i, 0)),
        ],
        out_specs=pl.BlockSpec((STEP, rows, LANES), lambda i: (i, 0, 0)),
        scratch_shapes=[
            pltpu.VMEM((2, depth, 2 * LANES), jnp.bfloat16),
            pltpu.VMEM((2, 2 * rows, depth), jnp.float32),
        ],
        compiler_params=pltpu.CompilerParams(vmem_limit_bytes=24 * 1024 * 1024),
        cost_estimate=pl.CostEstimate(
            flops=2 * 2 * rows * 2 * LANES * depth * channels,
            bytes_accessed=4 * channels * (depth + 2 * span + rows * LANES),
            transcendentals=0,
        ),
    )(grad_ext.astype(jnp.float32), turned(kernel_taps), turned(conv_input))
    result = out[:, :out_blocks].reshape(channels, tok_len)
    tap_sums = out[:, out_blocks : out_blocks + tap_blocks].reshape(channels, span)
    return result, tap_sums


def on_device(out_grad, out_weight, conv_input, gate_values, conv_output, filters, filter_reach):
    chan_rows = conv_input.shape[0]
    tok_len = conv_input.shape[1]
    tap_count = filters.shape[2]
    gated = (conv_output.astype(jnp.float32) * gate_values.astype(jnp.float32)).astype(jnp.bfloat16)
    gathered = lax.all_gather(gated, "chan", axis=0, tiled=True)
    partial = lax.dot_general(
        out_weight, out_grad, (((1,), (1,)), ((), ())), preferred_element_type=jnp.float32
    ).astype(jnp.bfloat16)
    partial, gathered = lax.optimization_barrier((partial, gathered))
    summed = lax.psum_scatter(partial, "chan", scatter_dimension=0, tiled=True)
    weight_term = jnp.dot(gathered, out_grad, preferred_element_type=jnp.float32)
    summed, weight_term = lax.optimization_barrier((summed, weight_term))
    grad_gated = summed.astype(jnp.float32)
    grad_gate = grad_gated * conv_output.astype(jnp.float32)
    grad_conv = (grad_gated * gate_values.astype(jnp.float32)).astype(jnp.bfloat16)
    grad_ext = extended(grad_conv, (("seq", 1),), tap_count)
    channel_ids = lax.axis_index("chan") * chan_rows + jnp.arange(chan_rows, dtype=jnp.int32)
    group_ids = channel_ids // GROUP
    levels = jnp.arange(filter_reach.shape[0], dtype=jnp.int32)
    reach_rows = jnp.sum(
        jnp.where(group_ids[:, None] == levels[None, :], filter_reach[None, :], 0), axis=1
    )
    inside = jnp.arange(tap_count, dtype=jnp.int32)[None, :] < reach_rows[:, None]
    nothing = jnp.zeros((), filters.dtype)
    ahead = jnp.where(inside, filters[0], nothing)
    behind = jnp.where(inside, filters[1], nothing)
    kernel_taps = jnp.concatenate([behind[:, ::-1], ahead], axis=1)
    grad_input, tap_sums = filter_terms(grad_ext, conv_input, kernel_taps)
    tap_grads = jnp.stack([tap_sums[:, tap_count:], tap_sums[:, :tap_count][:, ::-1]])
    tap_grads = tap_grads * inside[None].astype(jnp.float32)
    grad_scale = 1.0 / math.sqrt(tok_len * lax.axis_size("seq"))
    weight_sum, taps_sum = (
        lax.psum_scatter(weight_term, "seq", scatter_dimension=0, tiled=True),
        lax.psum_scatter(tap_grads, "seq", scatter_dimension=2, tiled=True),
    )
    return (grad_input, grad_gate, weight_sum * grad_scale, taps_sum * grad_scale)


def solution(mesh):
    return jax.shard_map(
        on_device,
        mesh=mesh,
        in_specs=(
            P("seq", "chan"),
            P(None, "chan"),
            P("chan", "seq"),
            P("chan", "seq"),
            P("chan", "seq"),
            P(None, "chan", None),
            P(),
        ),
        out_specs=(P("chan", "seq"), P("chan", "seq"), P("seq", "chan"), P(None, "chan", "seq")),
        check_vma=False,
    )
```

profile of v0, /device:TPU:0, one launch (start us, length us, event | category | flops | bytes accessed | tf_op | source)
XLA Modules:
  0.0 251.8 jit_solution(18009076351387827588)
XLA Ops:
  7.2 1.9 fusion
  9.3 5.6 %convolution_convert_fusion = bf16[1024,512]{1,0:T(8,128)(2,1)} fusion(bf16[1024,2048]{1,0:T(8,128)(2,1)} %param.8, bf16[512,2048]{1,0:T(8,128)(2,1)S(1)} %copy-done), kind=kOutput, calls=%fused_computation | convolution fusion | flops 2148007936 | bytes 7340032 | tf_op jit(solution)/shard_map/dot_general | solution.py:121
  14.8 26.0 %all-gather.2.cloned.1.call-done = bf16[1024,512]{1,0:T(8,128)(2,1)} async-done(((bf16[256,512]{1,0:T(8,128)(2,1)}), bf16[1024,512]{1,0:T(8,128)(2,1)}) %all-gather.2.cloned.1.call-update) | async-done | bytes 1048592 | tf_op jit(solution)/shard_map/all_gather | solution.py:120
  42.9 6.8 %fusion.5 = f32[1024,2048]{1,0:T(8,128)} fusion(bf16[1024,512]{1,0:T(8,128)(2,1)} %all-gather.2.cloned.1.call-done, bf16[512,2048]{1,0:T(8,128)(2,1)S(1)} %copy-done), kind=kOutput, calls=%fused_computation.25 | convolution fusion | flops 2147483648 | bytes 11534336 | tf_op jit(solution)/shard_map/dot_general | solution.py:126
  49.7 20.6 %reduce-scatter.4.cloned.1.call-done = bf16[256,512]{1,0:T(8,128)(2,1)} async-done(((bf16[1024,512]{1,0:T(8,128)(2,1)}), bf16[256,512]{1,0:T(8,128)(2,1)}) %reduce-scatter.4.cloned.1.call-update) | async-done | bytes 262160 | tf_op jit(solution)/shard_map/reduce_scatter | solution.py:125
  70.4 1.8 convert_multiply_fusion
  72.2 1.3 collective-permute-start.1
  73.5 3.8 %collective-permute-start = (bf16[256,512]{1,0:T(8,128)(2,1)S(1)}, bf16[256,512]{1,0:T(8,128)(2,1)}, u32[]{:S(2)}, u32[]{:S(2)}) collective-permute-start(bf16[256,512]{1,0:T(8,128)(2,1)S(1)} %get-tuple-element.17), channel_id=1, source_target_pairs={{0,4},{4,8},{8,12},{12,16},{16,20},{20,24},{24,28},{1,5},{5,9},{9,... | collective-permute-start | bytes 786440 | tf_op jit(solution)/shard_map/ppermute | solution.py:20
  77.3 1.2 fusion.4
  78.5 2.9 %rev.12 = bf16[256,512]{1,0:T(8,128)(2,1)} reverse(bf16[256,512]{1,0:T(8,128)(2,1)S(1)} %get-tuple-element.14), dimensions={1} | reverse | bytes 524288 | tf_op jit(solution)/shard_map/rev | solution.py:142
  83.3 1.3 rev.13
  84.8 1.2 maximum_convert_fusion.grad_ref
  86.0 36.3 %shard_map.102 = f32[256,16,128]{2,1,0:T(8,128)S(1)} custom-call(f32[256,1536]{1,0:T(8,128)S(1)} %maximum_convert_fusion.grad_ref, f32[256,1024]{1,0:T(8,128)S(1)} %bitcast.29, f32[256,512]{1,0:T(8,128)S(1)} %bitcast.30), custom_call_target="tpu_custom_call" | custom-call | flops 5905580032 | bytes 5636096 | tf_op jit(solution)/shard_map/pallas_call | solution.py:89
  122.3 1.4 copy-done.1
  123.7 1.1 slice.25
  124.7 1.6 copy.17
  126.3 1.0 slice_bitcast_fusion
  127.3 3.4 %rev.15 = f32[256,512]{0,1:T(8,128)S(1)} reverse(f32[256,512]{0,1:T(8,128)} %get-tuple-element.13), dimensions={1} | reverse | bytes 1048576 | tf_op jit(solution)/shard_map/rev | solution.py:144
  130.8 2.3 maximum_multiply_fusion
  133.6 1.3 slice.24
  135.8 32.2 %reduce-scatter.8.cloned.1.call-done = f32[2,256,64]{1,2,0:T(8,128)} async-done(((f32[2,256,512]{1,2,0:T(8,128)}), f32[2,256,64]{1,2,0:T(8,128)}) %reduce-scatter.8.cloned.1.call-update) | async-done | bytes 131088 | tf_op jit(solution)/shard_map/reduce_scatter | solution.py:149
  167.9 1.6 broadcast_multiply_fusion.1
  169.5 73.4 %reduce-scatter.6.cloned.1.call-done = f32[128,2048]{1,0:T(8,128)} async-done(((f32[1024,2048]{1,0:T(8,128)}), f32[128,2048]{1,0:T(8,128)}) %reduce-scatter.6.cloned.1.call-update) | async-done | bytes 1048592 | tf_op jit(solution)/shard_map/reduce_scatter | solution.py:148
  242.9 2.3 broadcast_multiply_fusion
  (32 shorter events, 5.5 us)
Async XLA Ops:
  7.2 2.1 copy-start
  7.2 33.6 %all-gather.2.cloned.1.call-start = ((), (), s32[]{:S(2)}) async-start(), calls=%async_computation.3 | async-start | bytes 1310720 | tf_op jit(solution)/shard_map/all_gather | solution.py:120
  9.2 31.7 %copy-start.4 = (bf16[256,512]{1,0:T(8,128)(2,1)S(1)}, bf16[256,512]{1,0:T(8,128)(2,1)}, u32[]{:S(2)}) copy-start(bf16[256,512]{1,0:T(8,128)(2,1)} %param.9) | copy-start | bytes 786436
  9.2 61.2 %reduce-scatter.4.cloned.1.call-start = ((), (), s32[]{:S(2)}) async-start(), calls=%async_computation.4 | async-start | bytes 1310720 | tf_op jit(solution)/shard_map/reduce_scatter | solution.py:125
  14.8 26.9 %copy-start.5 = (s32[16]{0:T(128)S(1)}, s32[16]{0:T(128)}, u32[]{:S(2)}) copy-start(s32[16]{0:T(128)} %param.13) | copy-start | bytes 196
  40.8 127.1 %reduce-scatter.8.cloned.1.call-start = ((), (), s32[]{:S(2)}) async-start(), calls=%async_computation.6 | async-start | bytes 1179648 | tf_op jit(solution)/shard_map/reduce_scatter | solution.py:149
  42.9 27.5 %copy-start.2 = (bf16[256,512]{1,0:T(8,128)(2,1)S(1)}, bf16[256,512]{1,0:T(8,128)(2,1)}, u32[]{:S(2)}) copy-start(bf16[256,512]{1,0:T(8,128)(2,1)} %param.10) | copy-start | bytes 786436
  42.9 27.5 %copy-start.3 = (bf16[256,512]{1,0:T(8,128)(2,1)S(1)}, bf16[256,512]{1,0:T(8,128)(2,1)}, u32[]{:S(2)}) copy-start(bf16[256,512]{1,0:T(8,128)(2,1)} %param.11) | copy-start | bytes 786436
  72.2 12.5 %collective-permute-start.1 = (bf16[256,512]{1,0:T(8,128)(2,1)S(1)}, bf16[256,512]{1,0:T(8,128)(2,1)}, u32[]{:S(2)}, u32[]{:S(2)}) collective-permute-start(bf16[256,512]{1,0:T(8,128)(2,1)S(1)} %get-tuple-element.17), channel_id=1, source_target_pairs={{4,0},{8,4},{12,8},{16,12},{20,16},{24,20},{28,24},{5,1},{9,5},{13... | collective-permute-start | bytes 786440 | tf_op jit(solution)/shard_map/ppermute | solution.py:23
  73.5 11.3 %collective-permute-start = (bf16[256,512]{1,0:T(8,128)(2,1)S(1)}, bf16[256,512]{1,0:T(8,128)(2,1)}, u32[]{:S(2)}, u32[]{:S(2)}) collective-permute-start(bf16[256,512]{1,0:T(8,128)(2,1)S(1)} %get-tuple-element.17), channel_id=1, source_target_pairs={{0,4},{4,8},{8,12},{12,16},{16,20},{20,24},{24,28},{1,5},{5,9},{9,... | collective-permute-start | bytes 786440 | tf_op jit(solution)/shard_map/ppermute | solution.py:20
  122.3 1.4 copy-start.1
  133.1 109.9 %reduce-scatter.6.cloned.1.call-start = ((), (), s32[]{:S(2)}) async-start(), calls=%async_computation.5 | async-start | bytes 9437184 | tf_op jit(solution)/shard_map/reduce_scatter | solution.py:148
Sparse Core Ops, SparseCore 0:
  10.2 30.6 all-gather.1
  43.7 26.6 reduce-scatter.3
  133.2 34.7 reduce-scatter.7
  171.6 71.2 reduce-scatter.5
where the time goes:
time: 252 us
  waiting for transfers between devices  153 us (61%)
  Pallas kernels  36.3 us (14%)
  local copies, waits for them, and re-layouts  17.6 us (7%)
  between operations  13.9 us (6%)
  other arithmetic  13.5 us (5%)
  matrix products  12.4 us (5%)
  starting transfers between devices  5.21 us (2%)
    reduce_scatter x1, waiting for transfers between devices, on_device(): lax.psum_scatter(weight_term, 'seq', scatter_dimension=0, tiled=True)  73.4 us
    pallas_call x1, Pallas kernels, filter_terms(): pl.pallas_call(correlate_kernel, grid=(channels // STEP,), out_shape=jax....  36.3 us
    reduce_scatter x1, waiting for transfers between devices, on_device(): lax.psum_scatter(tap_grads, 'seq', scatter_dimension=2, tiled=True)  32.2 us
    all_gather x1, waiting for transfers between devices, on_device(): gathered = lax.all_gather(gated, 'chan', axis=0, tiled=True)  26 us
    reduce_scatter x1, waiting for transfers between devices, on_device(): summed = lax.psum_scatter(partial, 'chan', scatter_dimension=0, tiled=True)  20.6 us
    dot_general x1, matrix products, on_device(): jnp.dot(gathered, out_grad, preferred_element_type=jnp.float32)  6.84 us
    dot_general x1, matrix products, on_device(): lax.dot_general(out_weight, out_grad, (((1,), (1,)), ((), ())), preferred...  5.55 us
  transfers between devices with their start and end apart: 6, of which 4 were waited for; matrix products, arithmetic and copies ran while one was open for 10% of the time, Pallas kernels for 0%

commit v1 on v0

--- a/solution.py
+++ b/solution.py
@@ -102,7 +102,7 @@
         ],
         compiler_params=pltpu.CompilerParams(vmem_limit_bytes=24 * 1024 * 1024),
         cost_estimate=pl.CostEstimate(
-            flops=2 * 2 * rows * 2 * LANES * depth * channels,
+            flops=8 * LANES * LANES * depth * channels,
             bytes_accessed=4 * channels * (depth + 2 * span + rows * LANES),
             transcendentals=0,
         ),
@@ -123,8 +123,9 @@
     ).astype(jnp.bfloat16)
     partial, gathered = lax.optimization_barrier((partial, gathered))
     summed = lax.psum_scatter(partial, "chan", scatter_dimension=0, tiled=True)
-    weight_term = jnp.dot(gathered, out_grad, preferred_element_type=jnp.float32)
+    weight_term = jnp.dot(gathered, out_grad, preferred_element_type=jnp.float32).astype(jnp.bfloat16)
     summed, weight_term = lax.optimization_barrier((summed, weight_term))
+    weight_sum = lax.psum_scatter(weight_term, "seq", scatter_dimension=0, tiled=True)
     grad_gated = summed.astype(jnp.float32)
     grad_gate = grad_gated * conv_output.astype(jnp.float32)
     grad_conv = (grad_gated * gate_values.astype(jnp.float32)).astype(jnp.bfloat16)
@@ -144,10 +145,11 @@
     tap_grads = jnp.stack([tap_sums[:, tap_count:], tap_sums[:, :tap_count][:, ::-1]])
     tap_grads = tap_grads * inside[None].astype(jnp.float32)
     grad_scale = 1.0 / math.sqrt(tok_len * lax.axis_size("seq"))
-    weight_sum, taps_sum = (
-        lax.psum_scatter(weight_term, "seq", scatter_dimension=0, tiled=True),
-        lax.psum_scatter(tap_grads, "seq", scatter_dimension=2, tiled=True),
+    tap_grads, weight_sum, grad_input = lax.optimization_barrier(
+        (tap_grads.astype(jnp.bfloat16), weight_sum, grad_input)
     )
+    taps_sum = lax.psum_scatter(tap_grads, "seq", scatter_dimension=2, tiled=True)
+    weight_sum, taps_sum = weight_sum.astype(jnp.float32), taps_sum.astype(jnp.float32)
     return (grad_input, grad_gate, weight_sum * grad_scale, taps_sum * grad_scale)
 
 

time: 252 us -> 176 us (0.70)
  waiting for transfers between devices: 153 us -> 81.4 us
  local copies, waits for them, and re-layouts: 17.6 us -> 14.8 us
    reduce_scatter x1, waiting for transfers between devices: 73.4 us -> 0.01 us  [on_device(): lax.psum_scatter(weight_term, 'seq', scatter_dimension=0, tiled=True)]
    reduce_scatter x1, waiting for transfers between devices: 20.6 us -> 23.2 us  [on_device(): summed = lax.psum_scatter(partial, 'chan', scatter_dimension=0, tiled=True)]
  transfers between devices with their start and end apart: 6 -> 6, of which waited for: 4 -> 3; matrix products, arithmetic and copies ran while one was open for 10% -> 20% of each run, Pallas kernels for 0% -> 21%
where the time goes in v1:
time: 176 us; the launch traced here: 175 us
  waiting for transfers between devices  81.4 us (46%)
  Pallas kernels  36.3 us (21%)
  local copies, waits for them, and re-layouts  14.8 us (8%)
  between operations  13.9 us (8%)
  other arithmetic  12.5 us (7%)
  matrix products  11.1 us (6%)
  starting transfers between devices  5.18 us (3%)
    pallas_call x1, Pallas kernels, filter_terms(): pl.pallas_call(correlate_kernel, grid=(channels // STEP,), out_shape=jax....  36.3 us
    reduce_scatter x1, waiting for transfers between devices, on_device(): lax.psum_scatter(tap_grads, 'seq', scatter_dimension=2, tiled=True)  32.1 us
    all_gather x1, waiting for transfers between devices, on_device(): gathered = lax.all_gather(gated, 'chan', axis=0, tiled=True)  26 us
    reduce_scatter x1, waiting for transfers between devices, on_device(): summed = lax.psum_scatter(partial, 'chan', scatter_dimension=0, tiled=True)  23.2 us
    dot_general x1, matrix products, on_device(): lax.dot_general(out_weight, out_grad, (((1,), (1,)), ((), ())), preferred...  5.55 us
    dot_general x1, matrix products, on_device(): jnp.dot(gathered, out_grad, preferred_element_type=jnp.float32)  5.52 us
    ppermute x1, starting transfers between devices, extended(): lax.ppermute(lax.slice_in_dim(block, block.shape[dim] - width, None, axis...  3.74 us
  transfers between devices with their start and end apart: 6, of which 3 were waited for; matrix products, arithmetic and copies ran while one was open for 20% of the time, Pallas kernels for 21%

profile of v1, /device:TPU:0, one launch (start us, length us, event | category | flops | bytes accessed | tf_op | source)
XLA Modules:
  0.0 175.2 jit_solution(11510855618444095923)
XLA Ops:
  7.2 1.9 %fusion.1 = bf16[256,512]{1,0:T(8,128)(2,1)} fusion(bf16[256,512]{1,0:T(8,128)(2,1)} %param.10, bf16[256,512]{1,0:T(8,128)(2,1)} %param.11), kind=kLoop, calls=%fused_computation.10 | loop fusion | flops 524288 | bytes 786432 | tf_op jit(solution)/shard_map/convert_element_type | solution.py:119
  9.3 5.6 %convolution_convert_fusion.1 = bf16[1024,512]{1,0:T(8,128)(2,1)} fusion(bf16[1024,2048]{1,0:T(8,128)(2,1)} %param.8, bf16[512,2048]{1,0:T(8,128)(2,1)S(1)} %copy-done), kind=kOutput, calls=%fused_computation.1 | convolution fusion | flops 2148007936 | bytes 7340032 | tf_op jit(solution)/shard_map/dot_general | solution.py:121
  14.8 26.0 %all-gather.2.cloned.1.call-done = bf16[1024,512]{1,0:T(8,128)(2,1)} async-done(((bf16[256,512]{1,0:T(8,128)(2,1)}), bf16[1024,512]{1,0:T(8,128)(2,1)}) %all-gather.2.cloned.1.call-update) | async-done | bytes 1048592 | tf_op jit(solution)/shard_map/all_gather | solution.py:120
  41.7 5.5 %convolution_convert_fusion = bf16[1024,2048]{1,0:T(8,128)(2,1)} fusion(bf16[1024,512]{1,0:T(8,128)(2,1)} %all-gather.2.cloned.1.call-done, bf16[512,2048]{1,0:T(8,128)(2,1)S(1)} %copy-done), kind=kOutput, calls=%fused_computation | convolution fusion | flops 2149580800 | bytes 7340032 | tf_op jit(solution)/shard_map/dot_general | solution.py:126
  47.2 23.2 %reduce-scatter.4.cloned.1.call-done = bf16[256,512]{1,0:T(8,128)(2,1)} async-done(((bf16[1024,512]{1,0:T(8,128)(2,1)}), bf16[256,512]{1,0:T(8,128)(2,1)}) %reduce-scatter.4.cloned.1.call-update) | async-done | bytes 262160 | tf_op jit(solution)/shard_map/reduce_scatter | solution.py:125
  70.7 1.0 copy.16
  71.7 2.0 %convert_multiply_fusion.1 = (f32[256,512]{1,0:T(8,128)}, bf16[256,512]{1,0:T(8,128)(2,1)}) fusion(bf16[256,512]{1,0:T(8,128)(2,1)} %reduce-scatter.4.cloned.1.call-done, bf16[256,512]{1,0:T(8,128)(2,1)} %param.11, bf16[256,512]{1,0:T(8,128)(2,1)S(1)} %copy-done.1), kind=kLoop, calls=%fused_computation.7 | loop fusion | flops 786432 | bytes 1572864 | tf_op jit(solution)/shard_map/mul | solution.py:130
  73.7 1.3 collective-permute-start.1
  75.0 3.7 %collective-permute-start = (bf16[256,512]{1,0:T(8,128)(2,1)}, bf16[256,512]{1,0:T(8,128)(2,1)}, u32[]{:S(2)}, u32[]{:S(2)}) collective-permute-start(bf16[256,512]{1,0:T(8,128)(2,1)} %get-tuple-element.23), channel_id=1, source_target_pairs={{0,4},{4,8},{8,12},{12,16},{16,20},{20,24},{24,28},{1,5},{5,9},{9,... | collective-permute-start | bytes 786440 | tf_op jit(solution)/shard_map/ppermute | solution.py:20
  78.7 1.2 fusion.5
  80.8 0.9 copy.18
  81.7 1.3 rev.13
  83.2 1.4 maximum_convert_fusion.grad_ref
  84.6 36.3 %shard_map.102 = f32[256,16,128]{2,1,0:T(8,128)S(1)} custom-call(f32[256,1536]{1,0:T(8,128)S(1)} %maximum_convert_fusion.grad_ref, f32[256,1024]{1,0:T(8,128)S(1)} %bitcast.29, f32[256,512]{1,0:T(8,128)S(1)} %bitcast.30), custom_call_target="tpu_custom_call" | custom-call | flops 47244640256 | bytes 5636096 | tf_op jit(solution)/shard_map/pallas_call | solution.py:89
  120.9 0.9 slice.27
  121.8 1.1 slice.24
  122.9 1.6 copy.17
  124.4 1.9 %copy.26 = f32[32,8,4,128]{3,1,2,0:T(8,128)} copy(f32[32,8,4,128]{3,2,1,0:T(4,128)} %bitcast.33) | data formatting | bytes 1048576
  126.3 1.1 slice_bitcast_fusion
  127.4 3.4 %rev.15 = f32[256,512]{0,1:T(8,128)S(1)} reverse(f32[256,512]{0,1:T(8,128)} %get-tuple-element.19), dimensions={1} | reverse | bytes 1048576 | tf_op jit(solution)/shard_map/rev | solution.py:145
  130.8 2.1 %fusion = bf16[2,256,512]{1,2,0:T(8,128)(2,1)} fusion(f32[1,256,512]{1,2,0:T(8,128)S(1)} %bitcast.35, f32[1,256,512]{1,2,0:T(8,128)} %get-tuple-element.18, f32[256,512]{0,1:T(8,128)} %copy.16), kind=kLoop, calls=%fused_computation.4 | loop fusion | flops 786432 | bytes 2097152 | tf_op jit(solution)/shard_map/convert_element_type | solution.py:149
  132.9 2.1 %convert_multiply_fusion = f32[128,2048]{1,0:T(8,128)} fusion(bf16[128,2048]{1,0:T(8,128)(2,1)} %reduce-scatter.6.cloned.1.call-done), kind=kLoop, calls=%fused_computation.5 | loop fusion | flops 524288 | bytes 1572864 | tf_op jit(solution)/shard_map/mul | solution.py:153
  135.1 32.1 %reduce-scatter.8.cloned.1.call-done = bf16[2,256,64]{1,2,0:T(8,128)(2,1)} async-done(((bf16[2,256,512]{1,2,0:T(8,128)(2,1)}), bf16[2,256,64]{1,2,0:T(8,128)(2,1)}) %reduce-scatter.8.cloned.1.call-update) | async-done | bytes 65552 | tf_op jit(solution)/shard_map/reduce_scatter | solution.py:151
  167.2 1.5 convert_multiply_fusion.4
  (28 shorter events, 2.2 us)
Async XLA Ops:
  7.2 2.1 %copy-start = (bf16[512,2048]{1,0:T(8,128)(2,1)S(1)}, bf16[512,2048]{1,0:T(8,128)(2,1)}, u32[]{:S(2)}) copy-start(bf16[512,2048]{1,0:T(8,128)(2,1)} %param.7) | copy-start | bytes 6291460
  7.2 33.6 %all-gather.2.cloned.1.call-start = ((), (), s32[]{:S(2)}) async-start(), calls=%async_computation.3 | async-start | bytes 1310720 | tf_op jit(solution)/shard_map/all_gather | solution.py:120
  9.2 31.7 %copy-start.2 = (bf16[256,512]{1,0:T(8,128)(2,1)S(1)}, bf16[256,512]{1,0:T(8,128)(2,1)}, u32[]{:S(2)}) copy-start(bf16[256,512]{1,0:T(8,128)(2,1)} %param.9) | copy-start | bytes 786436
  9.2 61.2 %reduce-scatter.4.cloned.1.call-start = ((), (), s32[]{:S(2)}) async-start(), calls=%async_computation.4 | async-start | bytes 1310720 | tf_op jit(solution)/shard_map/reduce_scatter | solution.py:125
  40.8 92.1 %reduce-scatter.6.cloned.1.call-start = ((), (), s32[]{:S(2)}) async-start(), calls=%async_computation.5 | async-start | bytes 4718592 | tf_op jit(solution)/shard_map/reduce_scatter | solution.py:128
  47.2 23.3 %copy-start.3 = (s32[16]{0:T(128)S(1)}, s32[16]{0:T(128)}, u32[]{:S(2)}) copy-start(s32[16]{0:T(128)} %param.13) | copy-start | bytes 196
  47.2 24.5 %copy-start.1 = (bf16[256,512]{1,0:T(8,128)(2,1)S(1)}, bf16[256,512]{1,0:T(8,128)(2,1)}, u32[]{:S(2)}) copy-start(bf16[256,512]{1,0:T(8,128)(2,1)} %param.10) | copy-start | bytes 786436
  70.4 96.8 %reduce-scatter.8.cloned.1.call-start = ((), (), s32[]{:S(2)}) async-start(), calls=%async_computation.6 | async-start | bytes 589824 | tf_op jit(solution)/shard_map/reduce_scatter | solution.py:151
  73.7 9.5 %collective-permute-start.1 = (bf16[256,512]{1,0:T(8,128)(2,1)}, bf16[256,512]{1,0:T(8,128)(2,1)}, u32[]{:S(2)}, u32[]{:S(2)}) collective-permute-start(bf16[256,512]{1,0:T(8,128)(2,1)} %get-tuple-element.23), channel_id=1, source_target_pairs={{4,0},{8,4},{12,8},{16,12},{20,16},{24,20},{28,24},{5,1},{9,5},{13... | collective-permute-start | bytes 786440 | tf_op jit(solution)/shard_map/ppermute | solution.py:23
  75.0 8.2 %collective-permute-start = (bf16[256,512]{1,0:T(8,128)(2,1)}, bf16[256,512]{1,0:T(8,128)(2,1)}, u32[]{:S(2)}, u32[]{:S(2)}) collective-permute-start(bf16[256,512]{1,0:T(8,128)(2,1)} %get-tuple-element.23), channel_id=1, source_target_pairs={{0,4},{4,8},{8,12},{12,16},{16,20},{20,24},{24,28},{1,5},{5,9},{9,... | collective-permute-start | bytes 786440 | tf_op jit(solution)/shard_map/ppermute | solution.py:20
Sparse Core Ops, SparseCore 0:
  10.2 30.6 all-gather.1
  43.7 26.6 reduce-scatter.3
  74.1 49.9 reduce-scatter.5
  133.1 34.0 reduce-scatter.7

commit v2 on v1

--- a/solution.py
+++ b/solution.py
@@ -23,6 +23,30 @@
         high = lax.ppermute(lax.slice_in_dim(block, 0, width, axis=dim), axis, backward)
         block = jnp.concatenate([low, block, high], axis=dim)
     return block
+
+
+def gather_rows(block, axis):
+    count, me = lax.axis_size(axis), lax.axis_index(axis)
+    rows = block.shape[0]
+    whole = jnp.zeros((count * rows, block.shape[1]), block.dtype)
+    whole = lax.dynamic_update_slice(whole, block, (me * rows, 0))
+    for step in range(1, count):
+        arrived = lax.ppermute(block, axis, [(i, (i + step) % count) for i in range(count)])
+        owner = lax.rem(me + count - step, count)
+        whole = lax.dynamic_update_slice(whole, arrived, (owner * rows, 0))
+    return whole
+
+
+def turned(array):
+    channels = array.shape[0]
+    return array.reshape(channels, -1, LANES)[:, :, ::-1].reshape(channels, -1)
+
+
+def pieces_reversed(array, width):
+    total = array.shape[1]
+    return jnp.concatenate(
+        [array[:, total - start - width : total - start] for start in range(0, total, width)], axis=1
+    )
 
 
 def correlate_kernel(grad_ref, taps_ref, input_ref, out_ref, tiles_ref, lines_ref):
@@ -74,17 +98,14 @@
         out_ref[2 * pair + 1] = product[rows:, LANES:]
 
 
-def filter_terms(grad_ext, conv_input, kernel_taps):
-    channels, tok_len = conv_input.shape
-    span = kernel_taps.shape[1]
+def filter_terms(grad_ext, input_turned, taps_turned):
+    channels, tok_len = input_turned.shape
+    span = taps_turned.shape[1]
     out_blocks = tok_len // LANES
     tap_blocks = span // LANES
     tile_count = out_blocks + tap_blocks - 1
     depth = tile_count * LANES
     rows = -(-(out_blocks + tap_blocks) // 16) * 16
-
-    def turned(array):
-        return array.reshape(channels, -1, LANES)[:, :, ::-1].reshape(channels, -1).astype(jnp.float32)
 
     out = pl.pallas_call(
         correlate_kernel,
@@ -106,7 +127,7 @@
             bytes_accessed=4 * channels * (depth + 2 * span + rows * LANES),
             transcendentals=0,
         ),
-    )(grad_ext.astype(jnp.float32), turned(kernel_taps), turned(conv_input))
+    )(grad_ext.astype(jnp.float32), taps_turned, input_turned)
     result = out[:, :out_blocks].reshape(channels, tok_len)
     tap_sums = out[:, out_blocks : out_blocks + tap_blocks].reshape(channels, span)
     return result, tap_sums
@@ -117,12 +138,12 @@
     tok_len = conv_input.shape[1]
     tap_count = filters.shape[2]
     gated = (conv_output.astype(jnp.float32) * gate_values.astype(jnp.float32)).astype(jnp.bfloat16)
-    gathered = lax.all_gather(gated, "chan", axis=0, tiled=True)
     partial = lax.dot_general(
         out_weight, out_grad, (((1,), (1,)), ((), ())), preferred_element_type=jnp.float32
     ).astype(jnp.bfloat16)
-    partial, gathered = lax.optimization_barrier((partial, gathered))
+    partial, gated = lax.optimization_barrier((partial, gated))
     summed = lax.psum_scatter(partial, "chan", scatter_dimension=0, tiled=True)
+    gathered = gather_rows(gated, "chan")
     weight_term = jnp.dot(gathered, out_grad, preferred_element_type=jnp.float32).astype(jnp.bfloat16)
     summed, weight_term = lax.optimization_barrier((summed, weight_term))
     weight_sum = lax.psum_scatter(weight_term, "seq", scatter_dimension=0, tiled=True)
@@ -140,16 +161,24 @@
     nothing = jnp.zeros((), filters.dtype)
     ahead = jnp.where(inside, filters[0], nothing)
     behind = jnp.where(inside, filters[1], nothing)
-    kernel_taps = jnp.concatenate([behind[:, ::-1], ahead], axis=1)
-    grad_input, tap_sums = filter_terms(grad_ext, conv_input, kernel_taps)
-    tap_grads = jnp.stack([tap_sums[:, tap_count:], tap_sums[:, :tap_count][:, ::-1]])
-    tap_grads = tap_grads * inside[None].astype(jnp.float32)
+    taps_turned = jnp.concatenate([pieces_reversed(behind, LANES), turned(ahead)], axis=1)
+    grad_input, tap_sums = filter_terms(
+        grad_ext, turned(conv_input).astype(jnp.float32), taps_turned.astype(jnp.float32)
+    )
+    width = tap_count // lax.axis_size("seq")
+    tap_grads = jnp.stack([tap_sums[:, tap_count:], pieces_reversed(tap_sums[:, :tap_count], width)])
     grad_scale = 1.0 / math.sqrt(tok_len * lax.axis_size("seq"))
     tap_grads, weight_sum, grad_input = lax.optimization_barrier(
         (tap_grads.astype(jnp.bfloat16), weight_sum, grad_input)
     )
     taps_sum = lax.psum_scatter(tap_grads, "seq", scatter_dimension=2, tiled=True)
     weight_sum, taps_sum = weight_sum.astype(jnp.float32), taps_sum.astype(jnp.float32)
+    own_taps = lax.axis_index("seq") * width + jnp.arange(width, dtype=jnp.int32)
+    taps_sum = jnp.where(
+        own_taps[None, None, :] < reach_rows[None, :, None],
+        jnp.stack([taps_sum[0], taps_sum[1][:, ::-1]]),
+        0.0,
+    )
     return (grad_input, grad_gate, weight_sum * grad_scale, taps_sum * grad_scale)
 
 

time: 176 us -> 180 us (1.023)
  starting transfers between devices: 5.18 us -> 11.2 us
  waiting for transfers between devices: 81.4 us -> 78.1 us
  local copies, waits for them, and re-layouts: 14.8 us -> 16.8 us
    ppermute x0 -> x3, waiting for transfers between devices: none -> 28.3 us  [gather_rows(): lax.ppermute(block, axis, [(i, (i + step) % count) for i in range(count)])]
    all_gather x1 -> x0, waiting for transfers between devices: 26 us -> none  [on_device(): gathered = lax.all_gather(gated, 'chan', axis=0, tiled=True)]
    reduce_scatter x1, waiting for transfers between devices: 23.2 us -> 0.01 us  [on_device(): summed = lax.psum_scatter(partial, 'chan', scatter_dimension=0, tiled=True)]
    reduce_scatter x1, waiting for transfers between devices: 0.01 us -> 14.8 us  [on_device(): lax.psum_scatter(weight_term, 'seq', scatter_dimension=0, tiled=True)]
    ppermute x0 -> x3, starting transfers between devices: none -> 6.06 us  [gather_rows(): lax.ppermute(block, axis, [(i, (i + step) % count) for i in range(count)])]
    rev x4 -> x3, local copies, waits for them, and re-layouts: 6.2 us -> 1.29 us  [the longest x2 1.21 us: turned(): return array.reshape(channels, -1, LANES)[:, :, ::-1].reshape(channels, -1)]
    dynamic_update_slice x0 -> x4, local copies, waits for them, and re-layouts: none -> 4.79 us  [the longest x3 4.08 us: gather_rows(): whole = lax.dynamic_update_slice(whole, arrived, (owner * rows, 0))]
    reduce_scatter x1, waiting for transfers between devices: 32.1 us -> 35 us  [on_device(): lax.psum_scatter(tap_grads, 'seq', scatter_dimension=2, tiled=True)]
  transfers between devices with their start and end apart: 6 -> 8, of which waited for: 3 -> 4; matrix products, arithmetic and copies ran while one was open for 20% -> 16% of each run, Pallas kernels for 21% -> 20%
where the time goes in v2:
time: 180 us; the launch traced here: 179 us
  waiting for transfers between devices  78.1 us (43%)
  Pallas kernels  36.3 us (20%)
  local copies, waits for them, and re-layouts  16.8 us (9%)
  between operations  14 us (8%)
  other arithmetic  11.6 us (6%)
  starting transfers between devices  11.2 us (6%)
  matrix products  11.1 us (6%)
    pallas_call x1, Pallas kernels, filter_terms(): pl.pallas_call(correlate_kernel, grid=(channels // STEP,), out_shape=jax....  36.3 us
    reduce_scatter x1, waiting for transfers between devices, on_device(): lax.psum_scatter(tap_grads, 'seq', scatter_dimension=2, tiled=True)  35 us
    ppermute x3, waiting for transfers between devices, gather_rows(): lax.ppermute(block, axis, [(i, (i + step) % count) for i in range(count)])  28.3 us
    reduce_scatter x1, waiting for transfers between devices, on_device(): lax.psum_scatter(weight_term, 'seq', scatter_dimension=0, tiled=True)  14.8 us
    ppermute x3, starting transfers between devices, gather_rows(): lax.ppermute(block, axis, [(i, (i + step) % count) for i in range(count)])  6.06 us
    dot_general x1, matrix products, on_device(): jnp.dot(gathered, out_grad, preferred_element_type=jnp.float32)  5.57 us
    dot_general x1, matrix products, on_device(): lax.dot_general(out_weight, out_grad, (((1,), (1,)), ((), ())), preferred...  5.56 us
    unnamed x23, local copies, waits for them, and re-layouts  4.75 us
  transfers between devices with their start and end apart: 8, of which 4 were waited for; matrix products, arithmetic and copies ran while one was open for 16% of the time, Pallas kernels for 20%

profile of v2, /device:TPU:0, one launch (start us, length us, event | category | flops | bytes accessed | tf_op | source)
XLA Modules:
  0.0 179.1 jit_solution(4149751021212887562)
XLA Ops:
  7.2 1.2 fusion
  8.9 5.6 %convolution_convert_fusion.1 = bf16[1024,512]{1,0:T(8,128)(2,1)} fusion(bf16[1024,2048]{1,0:T(8,128)(2,1)} %param.8, bf16[512,2048]{1,0:T(8,128)(2,1)S(1)} %copy-done), kind=kOutput, calls=%fused_computation.1 | convolution fusion | flops 2148007936 | bytes 7340032 | tf_op jit(solution)/shard_map/dot_general | solution.py:141
  14.5 5.1 %collective-permute-start.2 = (bf16[256,512]{1,0:T(8,128)(2,1)S(1)}, bf16[256,512]{1,0:T(8,128)(2,1)S(1)}, u32[]{:S(2)}, u32[]{:S(2)}) collective-permute-start(bf16[256,512]{1,0:T(8,128)(2,1)S(1)} %fusion), channel_id=1, source_target_pairs={{0,3},{1,0},{2,1},{3,2},{4,7},{5,4},{6,5},{7,6},{8,11},{9,8},{10,9... | collective-permute-start | bytes 786440 | tf_op jit(solution)/shard_map/ppermute | solution.py:34
  19.5 1.0 collective-permute-start
  20.8 1.1 fusion.2
  24.2 1.0 broadcast_in_dim.41
  25.9 20.9 %collective-permute-done = bf16[256,512]{1,0:T(8,128)(2,1)} collective-permute-done((bf16[256,512]{1,0:T(8,128)(2,1)S(1)}, bf16[256,512]{1,0:T(8,128)(2,1)}, u32[]{:S(2)}, u32[]{:S(2)}) %collective-permute-start) | collective-permute-done | bytes 262176 | tf_op jit(solution)/shard_map/ppermute | solution.py:34
  46.8 1.7 constant_dynamic-update-slice_fusion.2
  48.5 7.4 %collective-permute-done.1 = bf16[256,512]{1,0:T(8,128)(2,1)} collective-permute-done((bf16[256,512]{1,0:T(8,128)(2,1)S(1)}, bf16[256,512]{1,0:T(8,128)(2,1)}, u32[]{:S(2)}, u32[]{:S(2)}) %collective-permute-start.1) | collective-permute-done | bytes 262176 | tf_op jit(solution)/shard_map/ppermute | solution.py:34
  55.9 1.7 constant_dynamic-update-slice_fusion.1
  58.3 5.6 %convolution_convert_fusion = bf16[1024,2048]{1,0:T(8,128)(2,1)} fusion(bf16[1024,512]{1,0:T(8,128)(2,1)} %constant_dynamic-update-slice_fusion, bf16[512,2048]{1,0:T(8,128)(2,1)S(1)} %copy-done), kind=kOutput, calls=%fused_computation | convolution fusion | flops 2149580800 | bytes 7340032 | tf_op jit(solution)/shard_map/dot_general | solution.py:147
  63.9 1.9 %convert_multiply_fusion.1 = (f32[256,512]{1,0:T(8,128)}, bf16[256,512]{1,0:T(8,128)(2,1)S(1)}) fusion(bf16[256,512]{1,0:T(8,128)(2,1)} %reduce-scatter.4.cloned.1.call-done, bf16[256,512]{1,0:T(8,128)(2,1)S(1)} %copy-done.2, bf16[256,512]{1,0:T(8,128)(2,1)S(1)} %copy-done.3), kind=kLoop, calls=%fused_computation.5 | loop fusion | flops 786432 | bytes 1572864 | tf_op jit(solution)/shard_map/mul | solution.py:151
  65.7 1.3 collective-permute-start.4
  67.0 3.7 %collective-permute-start.3 = (bf16[256,512]{1,0:T(8,128)(2,1)S(1)}, bf16[256,512]{1,0:T(8,128)(2,1)}, u32[]{:S(2)}, u32[]{:S(2)}) collective-permute-start(bf16[256,512]{1,0:T(8,128)(2,1)S(1)} %get-tuple-element.19), channel_id=1, source_target_pairs={{0,4},{4,8},{8,12},{12,16},{16,20},{20,24},{24,28},{1,5},{5,9},{9,... | collective-permute-start | bytes 786440 | tf_op jit(solution)/shard_map/ppermute | solution.py:20
  71.4 1.0 reshape.95
  73.1 0.9 copy.37
  75.3 1.1 convert_element_type.49.taps_ref
  76.5 1.3 maximum_convert_fusion.grad_ref
  77.8 36.3 %shard_map.102 = f32[256,16,128]{2,1,0:T(8,128)S(1)} custom-call(f32[256,1536]{1,0:T(8,128)S(1)} %maximum_convert_fusion.grad_ref, f32[256,1024]{1,0:T(8,128)S(1)} %convert_element_type.49.taps_ref, f32[256,512]{1,0:T(8,128)S(1)} %bitcast.25), custom_call_target="tpu_custom_call" | custom-call | flops 47244640256 | bytes 5636096 | tf_op jit(solution)/shard_map/pallas_call | solution.py:110
  114.2 0.9 slice.127
  115.1 1.3 copy.29
  118.2 14.8 %reduce-scatter.6.cloned.1.call-done = bf16[128,2048]{1,0:T(8,128)(2,1)} async-done(((bf16[1024,2048]{1,0:T(8,128)(2,1)}), bf16[128,2048]{1,0:T(8,128)(2,1)}) %reduce-scatter.6.cloned.1.call-update) | async-done | bytes 524304 | tf_op jit(solution)/shard_map/reduce_scatter | solution.py:149
  133.1 2.1 %convert_multiply_fusion = f32[128,2048]{1,0:T(8,128)} fusion(bf16[128,2048]{1,0:T(8,128)(2,1)} %reduce-scatter.6.cloned.1.call-done), kind=kLoop, calls=%fused_computation.3 | loop fusion | flops 524288 | bytes 1572864 | tf_op jit(solution)/shard_map/mul | solution.py:182
  135.2 35.0 %reduce-scatter.8.cloned.1.call-done = bf16[2,256,64]{1,2,0:T(8,128)(2,1)} async-done(((bf16[2,256,512]{1,2,0:T(8,128)(2,1)}), bf16[2,256,64]{1,2,0:T(8,128)(2,1)}) %reduce-scatter.8.cloned.1.call-update) | async-done | bytes 65552 | tf_op jit(solution)/shard_map/reduce_scatter | solution.py:174
  (56 shorter events, 11.4 us)
Async XLA Ops:
  7.2 1.8 copy-start
  7.2 56.7 %reduce-scatter.4.cloned.1.call-start = ((), (), s32[]{:S(2)}) async-start(), calls=%async_computation.3 | async-start | bytes 1310720 | tf_op jit(solution)/shard_map/reduce_scatter | solution.py:145
  8.9 11.7 %slice-start = ((bf16[2,256,512]{2,1,0:T(8,128)(2,1)}), bf16[1,256,512]{2,1,0:T(8,128)(2,1)S(1)}, s32[]{:S(2)}) async-start(bf16[2,256,512]{2,1,0:T(8,128)(2,1)} %param.12), calls=%async_computation.6 | async-start | bytes 524288 | tf_op jit(solution)/shard_map/slice | solution.py:162
  14.5 6.3 %copy-start.4 = (s32[16]{0:T(128)S(1)}, s32[16]{0:T(128)}, u32[]{:S(2)}) copy-start(s32[16]{0:T(128)} %param.13) | copy-start | bytes 196
  14.5 43.1 %collective-permute-start.2 = (bf16[256,512]{1,0:T(8,128)(2,1)S(1)}, bf16[256,512]{1,0:T(8,128)(2,1)S(1)}, u32[]{:S(2)}, u32[]{:S(2)}) collective-permute-start(bf16[256,512]{1,0:T(8,128)(2,1)S(1)} %fusion), channel_id=1, source_target_pairs={{0,3},{1,0},{2,1},{3,2},{4,7},{5,4},{6,5},{7,6},{8,11},{9,8},{10,9... | collective-permute-start | bytes 786440 | tf_op jit(solution)/shard_map/ppermute | solution.py:34
  19.5 36.4 %collective-permute-start.1 = (bf16[256,512]{1,0:T(8,128)(2,1)S(1)}, bf16[256,512]{1,0:T(8,128)(2,1)}, u32[]{:S(2)}, u32[]{:S(2)}) collective-permute-start(bf16[256,512]{1,0:T(8,128)(2,1)S(1)} %fusion), channel_id=1, source_target_pairs={{0,2},{1,3},{2,0},{3,1},{4,6},{5,7},{6,4},{7,5},{8,10},{9,11},{10,... | collective-permute-start | bytes 786440 | tf_op jit(solution)/shard_map/ppermute | solution.py:34
  19.5 27.3 %collective-permute-start = (bf16[256,512]{1,0:T(8,128)(2,1)S(1)}, bf16[256,512]{1,0:T(8,128)(2,1)}, u32[]{:S(2)}, u32[]{:S(2)}) collective-permute-start(bf16[256,512]{1,0:T(8,128)(2,1)S(1)} %fusion), channel_id=1, source_target_pairs={{0,1},{1,2},{2,3},{3,0},{4,5},{5,6},{6,7},{7,4},{8,9},{9,10},{10,1... | collective-permute-start | bytes 786440 | tf_op jit(solution)/shard_map/ppermute | solution.py:34
  20.6 112.4 %reduce-scatter.6.cloned.1.call-start = ((), (), s32[]{:S(2)}) async-start(), calls=%async_computation.4 | async-start | bytes 4718592 | tf_op jit(solution)/shard_map/reduce_scatter | solution.py:149
  58.3 5.6 %copy-start.2 = (bf16[256,512]{1,0:T(8,128)(2,1)S(1)}, bf16[256,512]{1,0:T(8,128)(2,1)}, u32[]{:S(2)}) copy-start(bf16[256,512]{1,0:T(8,128)(2,1)} %param.11) | copy-start | bytes 786436
  58.3 5.6 %copy-start.3 = (bf16[256,512]{1,0:T(8,128)(2,1)S(1)}, bf16[256,512]{1,0:T(8,128)(2,1)}, u32[]{:S(2)}) copy-start(bf16[256,512]{1,0:T(8,128)(2,1)} %param.10) | copy-start | bytes 786436
  65.7 10.8 %collective-permute-start.4 = (bf16[256,512]{1,0:T(8,128)(2,1)S(1)}, bf16[256,512]{1,0:T(8,128)(2,1)}, u32[]{:S(2)}, u32[]{:S(2)}) collective-permute-start(bf16[256,512]{1,0:T(8,128)(2,1)S(1)} %get-tuple-element.19), channel_id=1, source_target_pairs={{4,0},{8,4},{12,8},{16,12},{20,16},{24,20},{28,24},{5,1},{9,5},{13... | collective-permute-start | bytes 786440 | tf_op jit(solution)/shard_map/ppermute | solution.py:23
  67.0 9.5 %collective-permute-start.3 = (bf16[256,512]{1,0:T(8,128)(2,1)S(1)}, bf16[256,512]{1,0:T(8,128)(2,1)}, u32[]{:S(2)}, u32[]{:S(2)}) collective-permute-start(bf16[256,512]{1,0:T(8,128)(2,1)S(1)} %get-tuple-element.19), channel_id=1, source_target_pairs={{0,4},{4,8},{8,12},{12,16},{16,20},{20,24},{24,28},{1,5},{5,9},{9,... | collective-permute-start | bytes 786440 | tf_op jit(solution)/shard_map/ppermute | solution.py:20
  76.4 93.8 %reduce-scatter.8.cloned.1.call-start = ((), (), s32[]{:S(2)}) async-start(), calls=%async_computation.5 | async-start | bytes 589824 | tf_op jit(solution)/shard_map/reduce_scatter | solution.py:174
  76.5 1.3 copy-start.1
Sparse Core Ops, SparseCore 0:
  20.7 38.7 reduce-scatter.3
  76.6 56.3 reduce-scatter.5
  136.1 34.1 reduce-scatter.7
